TPU v7x, 512 devices: a whole 4x4x16 slice. The times are simulated.
512 devices in a mesh: seq: 128 (over x_lo, y, z), ch: 4 (over x_hi, core).
Axes of the slice: x: 4 (x_hi: 2, x_lo: 2; x = x_hi * 2 + x_lo), y: 4, z: 16, core: 2. Of those that a mesh axis runs over, the one named last changes fastest.
Arguments:
- query_proj: float32 [64, 131072], P('ch', 'seq'), may hold values from -6 to 6
- key_proj: float32 [64, 131072], P('ch', 'seq'), may hold values from -6 to 6
- value_proj: float32 [64, 131072], P('ch', 'seq'), may hold values from -6 to 6
- filter_taps: float32 [64, 131072], P('ch', 'seq'), may hold values from -6 to 6
- out_cotangent: float32 [64, 131072], P('ch', 'seq'), may hold values from -6 to 6
Outputs:
- hyena_out: float32 [64, 131072], P('ch', 'seq')
- query_grad: float32 [64, 131072], P('ch', 'seq')
- key_grad: float32 [64, 131072], P('ch', 'seq')
- value_grad: float32 [64, 131072], P('ch', 'seq')
- filter_grad: float32 [64, 131072], P('ch', 'seq')
All inputs are finite; a program needn't handle non-finite values.
Results may differ from a plain program's by a relative error of at most 0.000098.
Values sent between devices are 32-bit elements; how exact they have to be, the bound alone decides.
A program may use at most 64 MiB of HBM per device.

v0:
```python
import math

import jax
import jax.numpy as jnp
import numpy as np
from jax import lax
from jax.experimental import pallas as pl
from jax.experimental.pallas import tpu as pltpu
from jax.sharding import PartitionSpec as P

MESH = pl.DeviceIdType.MESH
LANES = 128
ROWS = 8
ITEMS = 3


def split_np(matrix):
    high = matrix.astype(jnp.bfloat16)
    low = (matrix - high.astype(np.float64)).astype(jnp.bfloat16)
    return high, low


def tables(run):
    k1 = np.arange(run)[:, None]
    n1 = np.arange(run)[None, :]
    first = ((2 * k1 + 1) * n1 % (4 * run)) * (2.0 * math.pi / (4 * run))
    first = np.concatenate([np.cos(first), -np.sin(first)], axis=0)
    n2 = np.arange(LANES)[None, :]
    turn = ((2 * k1 + 1) * n2) * (2.0 * math.pi / (4 * run * LANES))
    square = (np.arange(LANES)[:, None] * n2 % LANES) * (2.0 * math.pi / LANES)
    cos, sin = np.cos(square), np.sin(square)
    second = np.block([[cos, -sin], [sin, cos]])
    return (
        *split_np(first),
        np.cos(turn).astype(np.float32),
        (-np.sin(turn)).astype(np.float32),
        *split_np(second),
        *split_np(second.T),
        *split_np(first.T),
    )


def split(value):
    high = value.astype(jnp.bfloat16)
    low = (value - high.astype(jnp.float32)).astype(jnp.bfloat16)
    return high, low


def dot(left, right):
    return jnp.dot(left, right, preferred_element_type=jnp.float32)


def dot3(left, right):
    return dot(left[0], right[0]) + (dot(left[0], right[1]) + dot(left[1], right[0]))


def kernel(
    zs,
    bs,
    scale,
    q_hbm,
    k_hbm,
    v_hbm,
    f_hbm,
    o_hbm,
    *rest,
):
    table_hbm = rest[:10]
    out_refs = rest[10:15]
    (
        q_ref,
        k_ref,
        v_ref,
        f_ref,
        o_ref,
        *table_refs,
    ) = rest[15:30]
    (
        a_send,
        a_recv,
        b_send,
        b_recv,
        c_send,
        c_recv,
        d_send,
        d_recv,
        in_sem,
        send_sem,
        recv_sem,
    ) = rest[30:]
    run = zs * ROWS
    part = run // bs
    me = lax.axis_index("seq")
    block = me // zs
    lane = me % zs

    def z_peer(step):
        return lax.rem(lane + step, zs)

    def b_peer(step):
        return lax.rem(block + step, bs)

    barrier = pltpu.get_barrier_semaphore()

    @pl.loop(1, zs)
    def _(step):
        pl.semaphore_signal(
            barrier, inc=1, device_id={"seq": block * zs + z_peer(step)}, device_id_type=MESH
        )

    @pl.loop(1, bs)
    def _(step):
        pl.semaphore_signal(
            barrier, inc=1, device_id={"seq": b_peer(step) * zs + lane}, device_id_type=MESH
        )

    loads = [
        pltpu.make_async_copy(src, dst, in_sem.at[at])
        for at, (src, dst) in enumerate(
            zip(
                (k_hbm, v_hbm, f_hbm, o_hbm, q_hbm) + tuple(table_hbm),
                (k_ref, v_ref, f_ref, o_ref, q_ref) + tuple(table_refs),
            )
        )
    ]
    for load in loads:
        load.start()

    def fill(item, value):
        for row in range(ROWS):
            a_send[item, :, row, :] = value[:, row * LANES : (row + 1) * LANES]
        a_recv[item, lane] = a_send[item, lane]

    def spread_z(phase, item, source, target):
        @pl.loop(1, zs)
        def _(step):
            peer = z_peer(step)
            pltpu.make_async_remote_copy(
                src_ref=source.at[item, peer],
                dst_ref=target.at[item, lane],
                send_sem=send_sem.at[phase, item],
                recv_sem=recv_sem.at[phase, item],
                device_id={"seq": block * zs + peer},
                device_id_type=MESH,
            ).start()

    def spread_b(phase, item, source, target):
        @pl.loop(1, bs)
        def _(step):
            peer = b_peer(step)
            pltpu.make_async_remote_copy(
                src_ref=source.at[item, peer],
                dst_ref=target.at[item, block],
                send_sem=send_sem.at[phase, item],
                recv_sem=recv_sem.at[phase, item],
                device_id={"seq": peer * zs + lane},
                device_id_type=MESH,
            ).start()

    def await_all(sems, phase, item, buffer, count):
        whole = buffer.at[item, pl.ds(0, count - 1)]
        pltpu.make_async_copy(whole, whole, sems.at[phase, item]).wait()

    loads[0].wait()
    loads[1].wait()
    fill(0, k_ref[...] * v_ref[...])
    loads[2].wait()
    fill(1, f_ref[...])
    loads[3].wait()
    loads[4].wait()
    fill(2, o_ref[...] * q_ref[...])
    pl.semaphore_wait(barrier, zs - 1 + bs - 1)
    for item in range(ITEMS):
        spread_z(0, item, a_send, a_recv)
    for load in loads[5:]:
        load.wait()
    first = (table_refs[0], table_refs[1])
    turn_real, turn_imag = table_refs[2], table_refs[3]
    second = (table_refs[4], table_refs[5])
    second_back = (table_refs[6], table_refs[7])
    first_back = (table_refs[8], table_refs[9])

    def pair(refs):
        return refs[0][...], refs[1][...]

    def forward(item):
        await_all(recv_sem, 0, item, a_recv, zs)
        rows = a_recv[item].reshape(run, LANES)
        sums = dot3(pair(first), split(rows))
        real, imag = sums[:run], sums[run:]
        cos, sin = turn_real[...], turn_imag[...]
        turned = jnp.concatenate([real * cos - imag * sin, real * sin + imag * cos], axis=1)
        bins = dot3(split(turned), pair(second))
        b_send[item, :, 0] = bins[:, :LANES].reshape(bs, part, LANES)
        b_send[item, :, 1] = bins[:, LANES:].reshape(bs, part, LANES)
        b_recv[item, block] = b_send[item, block]
        spread_b(1, item, b_send, b_recv)

    sign = 1.0 - 2.0 * (lax.broadcasted_iota(jnp.int32, (part, LANES), 0) % 2).astype(jnp.float32)

    def spectrum(item, at):
        return b_recv[item, at, 0], b_recv[item, at, 1]

    def finish(item, sums, step, factor):
        for at in range(bs):
            real, imag = sums[at]
            other = at + step
            if 0 <= other < bs:
                over_real, over_imag = sums[other]
                real = real - factor * over_imag
                imag = imag + factor * over_real
            c_send[item, at, 0] = real
            c_send[item, at, 1] = imag
        c_recv[item, block] = c_send[item, block]
        spread_b(2, item, c_send, c_recv)

    def convolve(item, left, right):
        sums = []
        for at in range(bs):
            real = imag = None
            for of in range(at + 1):
                lr, li = spectrum(left, at - of)
                rr, ri = spectrum(right, of)
                pr, pi = lr * rr - li * ri, lr * ri + li * rr
                real, imag = (pr, pi) if real is None else (real + pr, imag + pi)
            sums.append((real, imag))
        finish(item, sums, -1, sign)

    def correlate(item, left, right):
        sums = []
        for at in range(bs):
            real = imag = None
            for of in range(bs - at):
                lr, li = spectrum(left, of)
                rr, ri = spectrum(right, at + of)
                pr, pi = lr * rr + li * ri, lr * ri - li * rr
                real, imag = (pr, pi) if real is None else (real + pr, imag + pi)
            sums.append((real, imag))
        finish(item, sums, 1, -sign)

    def inverse(item):
        await_all(recv_sem, 2, item, c_recv, bs)
        bins = jnp.concatenate(
            [c_recv[item, :, 0].reshape(run, LANES), c_recv[item, :, 1].reshape(run, LANES)], axis=1
        )
        sums = dot3(split(bins), pair(second_back))
        real, imag = sums[:, :LANES], sums[:, LANES:]
        cos, sin = turn_real[...], turn_imag[...]
        turned = jnp.concatenate([real * cos + imag * sin, imag * cos - real * sin], axis=0)
        rows = dot3(pair(first_back), split(turned)) * scale
        d_send[item] = rows.reshape(zs, ROWS, LANES)
        d_recv[item, lane] = d_send[item, lane]
        spread_z(3, item, d_send, d_recv)

    forward(0)
    forward(1)
    forward(2)
    await_all(recv_sem, 1, 0, b_recv, bs)
    await_all(recv_sem, 1, 1, b_recv, bs)
    convolve(0, 1, 0)
    await_all(recv_sem, 1, 2, b_recv, bs)
    correlate(1, 1, 2)
    correlate(2, 0, 2)
    inverse(0)
    inverse(1)
    inverse(2)

    for item in range(ITEMS):
        await_all(send_sem, 0, item, a_send, zs)
        await_all(send_sem, 1, item, b_send, bs)
        await_all(send_sem, 2, item, c_send, bs)
    await_all(recv_sem, 3, 0, d_recv, zs)
    for row in range(ROWS):
        here = slice(row * LANES, (row + 1) * LANES)
        mixed = d_recv[0, :, row, :]
        out_refs[0][:, here] = q_ref[:, here] * mixed
        out_refs[1][:, here] = o_ref[:, here] * mixed
    await_all(recv_sem, 3, 1, d_recv, zs)
    for row in range(ROWS):
        here = slice(row * LANES, (row + 1) * LANES)
        gated_grad = d_recv[1, :, row, :]
        out_refs[2][:, here] = gated_grad * v_ref[:, here]
        out_refs[3][:, here] = gated_grad * k_ref[:, here]
    await_all(recv_sem, 3, 2, d_recv, zs)
    for row in range(ROWS):
        out_refs[4][:, row * LANES : (row + 1) * LANES] = d_recv[2, :, row, :]
    for item in range(ITEMS):
        await_all(send_sem, 3, item, d_send, zs)


def per_device(query_proj, key_proj, value_proj, filter_taps, out_cotangent):
    devices = lax.axis_size("seq")
    channels, tokens = filter_taps.shape
    zs = channels
    bs = devices // zs
    run = zs * ROWS
    part = run // bs
    scale = 1.0 / (run * LANES * math.sqrt(tokens * devices))
    table = tables(run)
    shape = jax.ShapeDtypeStruct((channels, tokens), jnp.float32)
    z_buffer = pltpu.VMEM((ITEMS, zs, ROWS, LANES), jnp.float32)
    b_buffer = pltpu.VMEM((ITEMS, bs, 2, part, LANES), jnp.float32)
    body = lambda *refs: kernel(zs, bs, scale, *refs)
    outs = pl.pallas_call(
        body,
        out_shape=[shape] * 5,
        in_specs=[pl.BlockSpec(memory_space=pl.ANY)] * (5 + len(table)),
        out_specs=[pl.BlockSpec(memory_space=pltpu.VMEM)] * 5,
        scratch_shapes=[
            *[pltpu.VMEM((channels, tokens), jnp.float32) for _ in range(5)],
            *[pltpu.VMEM(entry.shape, entry.dtype) for entry in table],
            z_buffer,
            z_buffer,
            b_buffer,
            b_buffer,
            b_buffer,
            b_buffer,
            z_buffer,
            z_buffer,
            pltpu.SemaphoreType.DMA((5 + len(table),)),
            pltpu.SemaphoreType.DMA((4, ITEMS)),
            pltpu.SemaphoreType.DMA((4, ITEMS)),
        ],
        compiler_params=pltpu.CompilerParams(
            collective_id=0, has_side_effects=True, vmem_limit_bytes=32 * 1024 * 1024
        ),
    )(
        query_proj,
        key_proj,
        value_proj,
        filter_taps,
        out_cotangent,
        *[jnp.asarray(entry) for entry in table],
    )
    return tuple(outs)


def solution(mesh):
    placed = (P("ch", "seq"),) * 5
    return jax.shard_map(
        per_device, mesh=mesh, in_specs=placed, out_specs=placed, check_vma=False
    )
```

profile of v0, /device:TPU:2, one launch (start us, length us, event | category | flops | bytes accessed | tf_op | source)
XLA Modules:
  0.0 66.4 jit_solution(9378514311643347109)
XLA Ops:
  0.6 0.0 copy-start
  0.6 0.9 %copy-done = bf16[256,256]{1,0:T(8,128)(2,1)S(1)} copy-done((bf16[256,256]{1,0:T(8,128)(2,1)S(1)}, bf16[256,256]{1,0:T(8,128)(2,1)}, u32[]{:S(2)}) %copy-start) | copy-done | bytes 131096
  1.5 0.0 copy-start.1
  1.5 0.9 %copy-done.1 = bf16[256,256]{1,0:T(8,128)(2,1)S(1)} copy-done((bf16[256,256]{1,0:T(8,128)(2,1)S(1)}, bf16[256,256]{1,0:T(8,128)(2,1)}, u32[]{:S(2)}) %copy-start.1) | copy-done | bytes 131096
  2.4 0.0 copy-start.2
  2.4 0.9 %copy-done.2 = bf16[256,256]{1,0:T(8,128)(2,1)S(1)} copy-done((bf16[256,256]{1,0:T(8,128)(2,1)S(1)}, bf16[256,256]{1,0:T(8,128)(2,1)}, u32[]{:S(2)}) %copy-start.2) | copy-done | bytes 131096
  3.4 0.0 copy-start.3
  3.4 0.9 %copy-done.3 = bf16[256,256]{1,0:T(8,128)(2,1)S(1)} copy-done((bf16[256,256]{1,0:T(8,128)(2,1)S(1)}, bf16[256,256]{1,0:T(8,128)(2,1)}, u32[]{:S(2)}) %copy-start.3) | copy-done | bytes 131096
  4.3 0.0 copy-start.4
  4.3 0.8 %copy-done.4 = f32[16,1024]{1,0:T(8,128)S(1)} copy-done((f32[16,1024]{1,0:T(8,128)S(1)}, f32[16,1024]{1,0:T(8,128)}, u32[]{:S(2)}) %copy-start.4) | copy-done | bytes 65560
  5.1 0.0 copy-start.5
  5.1 0.8 %copy-done.5 = f32[16,1024]{1,0:T(8,128)S(1)} copy-done((f32[16,1024]{1,0:T(8,128)S(1)}, f32[16,1024]{1,0:T(8,128)}, u32[]{:S(2)}) %copy-start.5) | copy-done | bytes 65560
  5.9 0.0 copy-start.6
  5.9 0.8 %copy-done.6 = f32[16,1024]{1,0:T(8,128)S(1)} copy-done((f32[16,1024]{1,0:T(8,128)S(1)}, f32[16,1024]{1,0:T(8,128)}, u32[]{:S(2)}) %copy-start.6) | copy-done | bytes 65560
  6.8 0.0 copy-start.7
  6.8 0.8 %copy-done.7 = f32[16,1024]{1,0:T(8,128)S(1)} copy-done((f32[16,1024]{1,0:T(8,128)S(1)}, f32[16,1024]{1,0:T(8,128)}, u32[]{:S(2)}) %copy-start.7) | copy-done | bytes 65560
  7.6 0.0 copy-start.8
  7.6 0.8 %copy-done.8 = f32[16,1024]{1,0:T(8,128)S(1)} copy-done((f32[16,1024]{1,0:T(8,128)S(1)}, f32[16,1024]{1,0:T(8,128)}, u32[]{:S(2)}) %copy-start.8) | copy-done | bytes 65560
  8.5 0.0 copy-start.9
  8.5 0.8 %copy-done.9 = bf16[128,256]{1,0:T(8,128)(2,1)S(1)} copy-done((bf16[128,256]{1,0:T(8,128)(2,1)S(1)}, bf16[128,256]{1,0:T(8,128)(2,1)}, u32[]{:S(2)}) %copy-start.9) | copy-done | bytes 65560
  9.3 0.0 copy-start.10
  9.3 0.8 %copy-done.10 = bf16[128,256]{1,0:T(8,128)(2,1)S(1)} copy-done((bf16[128,256]{1,0:T(8,128)(2,1)S(1)}, bf16[128,256]{1,0:T(8,128)(2,1)}, u32[]{:S(2)}) %copy-start.10) | copy-done | bytes 65560
  10.1 0.8 %copy-done.11 = f32[128,128]{1,0:T(8,128)S(1)} copy-done((f32[128,128]{1,0:T(8,128)S(1)}, f32[128,128]{1,0:T(8,128)}, u32[]{:S(2)}) %copy-start.11) | copy-done | bytes 65560
  11.0 0.8 %copy-done.12 = f32[128,128]{1,0:T(8,128)S(1)} copy-done((f32[128,128]{1,0:T(8,128)S(1)}, f32[128,128]{1,0:T(8,128)}, u32[]{:S(2)}) %copy-start.12) | copy-done | bytes 65560
  11.8 0.8 %copy-done.13 = bf16[256,128]{1,0:T(8,128)(2,1)S(1)} copy-done((bf16[256,128]{1,0:T(8,128)(2,1)S(1)}, bf16[256,128]{1,0:T(8,128)(2,1)}, u32[]{:S(2)}) %copy-start.13) | copy-done | bytes 65560
  12.7 0.8 %copy-done.14 = bf16[256,128]{1,0:T(8,128)(2,1)S(1)} copy-done((bf16[256,128]{1,0:T(8,128)(2,1)S(1)}, bf16[256,128]{1,0:T(8,128)(2,1)}, u32[]{:S(2)}) %copy-start.14) | copy-done | bytes 65560
  13.5 49.8 %shard_map.182 = (f32[16,1024]{1,0:T(8,128)S(1)}, f32[16,1024]{1,0:T(8,128)S(1)}, f32[16,1024]{1,0:T(8,128)S(1)}, f32[16,1024]{1,0:T(8,128)S(1)}, f32[16,1024]{1,0:T(8,128)S(1)}) custom-call(f32[16,1024]{1,0:T(8,128)S(1)} %copy-done.4, f32[16,1024]{1,0:T(8,128)S(1)} %copy-done.5, f32[16,1024]{1,0:T(8,128)S(1)} %copy-done.6, f32[16,1024]{1,0:T(8,128)S(1)} %copy-done.7, ...), custom_call_target="tpu_custom_call" | custom-call | tf_op jit(solution)/shard_map/pallas_call | solution.py:304
  63.3 0.6 copy.25
  63.9 0.6 copy.26
  64.5 0.6 copy.27
  65.2 0.6 copy.28
  65.8 0.6 copy.29
  (4 shorter events, 0.0 us)
Async XLA Ops:
  0.6 0.9 %copy-start = (bf16[256,256]{1,0:T(8,128)(2,1)S(1)}, bf16[256,256]{1,0:T(8,128)(2,1)}, u32[]{:S(2)}) copy-start(bf16[256,256]{1,0:T(8,128)(2,1)} %constant.27.clone.refs_12_) | copy-start | bytes 393220
  1.5 0.9 %copy-start.1 = (bf16[256,256]{1,0:T(8,128)(2,1)S(1)}, bf16[256,256]{1,0:T(8,128)(2,1)}, u32[]{:S(2)}) copy-start(bf16[256,256]{1,0:T(8,128)(2,1)} %constant.26.clone.refs_11_) | copy-start | bytes 393220
  2.4 0.9 %copy-start.2 = (bf16[256,256]{1,0:T(8,128)(2,1)S(1)}, bf16[256,256]{1,0:T(8,128)(2,1)}, u32[]{:S(2)}) copy-start(bf16[256,256]{1,0:T(8,128)(2,1)} %constant.25.clone.refs_10_) | copy-start | bytes 393220
  3.4 0.9 %copy-start.3 = (bf16[256,256]{1,0:T(8,128)(2,1)S(1)}, bf16[256,256]{1,0:T(8,128)(2,1)}, u32[]{:S(2)}) copy-start(bf16[256,256]{1,0:T(8,128)(2,1)} %constant.24.clone.refs_9_) | copy-start | bytes 393220
  4.3 0.8 %copy-start.4 = (f32[16,1024]{1,0:T(8,128)S(1)}, f32[16,1024]{1,0:T(8,128)}, u32[]{:S(2)}) copy-start(f32[16,1024]{1,0:T(8,128)} %refs_0_.1) | copy-start | bytes 196612
  5.1 0.8 %copy-start.5 = (f32[16,1024]{1,0:T(8,128)S(1)}, f32[16,1024]{1,0:T(8,128)}, u32[]{:S(2)}) copy-start(f32[16,1024]{1,0:T(8,128)} %refs_1_.1) | copy-start | bytes 196612
  5.9 0.8 %copy-start.6 = (f32[16,1024]{1,0:T(8,128)S(1)}, f32[16,1024]{1,0:T(8,128)}, u32[]{:S(2)}) copy-start(f32[16,1024]{1,0:T(8,128)} %refs_2_.1) | copy-start | bytes 196612
  6.8 0.8 %copy-start.7 = (f32[16,1024]{1,0:T(8,128)S(1)}, f32[16,1024]{1,0:T(8,128)}, u32[]{:S(2)}) copy-start(f32[16,1024]{1,0:T(8,128)} %refs_3_.1) | copy-start | bytes 196612
  7.6 0.8 %copy-start.8 = (f32[16,1024]{1,0:T(8,128)S(1)}, f32[16,1024]{1,0:T(8,128)}, u32[]{:S(2)}) copy-start(f32[16,1024]{1,0:T(8,128)} %refs_4_.1) | copy-start | bytes 196612
  8.5 0.8 %copy-start.9 = (bf16[128,256]{1,0:T(8,128)(2,1)S(1)}, bf16[128,256]{1,0:T(8,128)(2,1)}, u32[]{:S(2)}) copy-start(bf16[128,256]{1,0:T(8,128)(2,1)} %constant.29.clone.refs_14_) | copy-start | bytes 196612
  9.3 0.8 %copy-start.10 = (bf16[128,256]{1,0:T(8,128)(2,1)S(1)}, bf16[128,256]{1,0:T(8,128)(2,1)}, u32[]{:S(2)}) copy-start(bf16[128,256]{1,0:T(8,128)(2,1)} %constant.28.clone.refs_13_) | copy-start | bytes 196612
  10.1 0.8 %copy-start.11 = (f32[128,128]{1,0:T(8,128)S(1)}, f32[128,128]{1,0:T(8,128)}, u32[]{:S(2)}) copy-start(f32[128,128]{1,0:T(8,128)} %constant.23.clone.refs_8_) | copy-start | bytes 196612
  11.0 0.8 %copy-start.12 = (f32[128,128]{1,0:T(8,128)S(1)}, f32[128,128]{1,0:T(8,128)}, u32[]{:S(2)}) copy-start(f32[128,128]{1,0:T(8,128)} %constant.22.clone.refs_7_) | copy-start | bytes 196612
  11.8 0.8 %copy-start.13 = (bf16[256,128]{1,0:T(8,128)(2,1)S(1)}, bf16[256,128]{1,0:T(8,128)(2,1)}, u32[]{:S(2)}) copy-start(bf16[256,128]{1,0:T(8,128)(2,1)} %constant.21.clone.refs_6_) | copy-start | bytes 196612
  12.7 0.8 %copy-start.14 = (bf16[256,128]{1,0:T(8,128)(2,1)S(1)}, bf16[256,128]{1,0:T(8,128)(2,1)}, u32[]{:S(2)}) copy-start(bf16[256,128]{1,0:T(8,128)(2,1)} %constant.20.clone.refs_5_) | copy-start | bytes 196612
where the time goes:
time: 67.1 us; the launch traced here: 66.4 us
  Pallas kernels  49.8 us (74%)
  local copies, waits for them, and re-layouts  16 us (24%)
    pallas_call x1, Pallas kernels, per_device(): pl.pallas_call(body, out_shape=[shape] * 5, in_specs=[pl.BlockSpec(memory...  49.8 us
    unnamed x35, local copies, waits for them, and re-layouts  16 us

commit v1 on v0

--- a/solution.py
+++ b/solution.py
@@ -54,6 +54,17 @@
     return dot(left[0], right[0]) + (dot(left[0], right[1]) + dot(left[1], right[0]))
 
 
+def z_order(count):
+    near = [step for half in range((count - 1) // 2, 0, -1) for step in (half, count - half)]
+    return ([count // 2] if count % 2 == 0 else []) + near
+
+
+def b_order(count):
+    wide = count // 2
+    steps = [(dx, dy) for dx in range(2) for dy in range(wide) if dx or dy]
+    return sorted(steps, key=lambda step: -(step[0] + min(step[1], wide - step[1])))
+
+
 def kernel(
     zs,
     bs,
@@ -66,7 +77,7 @@
     *rest,
 ):
     table_hbm = rest[:10]
-    out_refs = rest[10:15]
+    out_hbm = rest[10]
     (
         q_ref,
         k_ref,
@@ -74,7 +85,7 @@
         f_ref,
         o_ref,
         *table_refs,
-    ) = rest[15:30]
+    ) = rest[11:26]
     (
         a_send,
         a_recv,
@@ -84,10 +95,12 @@
         c_recv,
         d_send,
         d_recv,
+        out_ref,
         in_sem,
+        out_sem,
         send_sem,
         recv_sem,
-    ) = rest[30:]
+    ) = rest[26:]
     run = zs * ROWS
     part = run // bs
     me = lax.axis_index("seq")
@@ -98,18 +111,16 @@
         return lax.rem(lane + step, zs)
 
     def b_peer(step):
-        return lax.rem(block + step, bs)
+        wide = bs // 2
+        across = lax.rem(lax.div(block, wide) + step[0], 2)
+        return across * wide + lax.rem(lax.rem(block, wide) + step[1], wide)
 
     barrier = pltpu.get_barrier_semaphore()
-
-    @pl.loop(1, zs)
-    def _(step):
+    for step in z_order(zs):
         pl.semaphore_signal(
             barrier, inc=1, device_id={"seq": block * zs + z_peer(step)}, device_id_type=MESH
         )
-
-    @pl.loop(1, bs)
-    def _(step):
+    for step in b_order(bs):
         pl.semaphore_signal(
             barrier, inc=1, device_id={"seq": b_peer(step) * zs + lane}, device_id_type=MESH
         )
@@ -128,12 +139,27 @@
 
     def fill(item, value):
         for row in range(ROWS):
-            a_send[item, :, row, :] = value[:, row * LANES : (row + 1) * LANES]
-        a_recv[item, lane] = a_send[item, lane]
+            a_send[:, item, row, :] = value[:, row * LANES : (row + 1) * LANES]
+        a_recv[lane, item] = a_send[lane, item]
+
+    def spread_a(group, items):
+        for step in z_order(zs):
+            peer = z_peer(step)
+            pltpu.make_async_remote_copy(
+                src_ref=a_send.at[peer, items],
+                dst_ref=a_recv.at[lane, items],
+                send_sem=send_sem.at[0, group],
+                recv_sem=recv_sem.at[0, group],
+                device_id={"seq": block * zs + peer},
+                device_id_type=MESH,
+            ).start()
+
+    def await_a(sems, group, items, buffer):
+        whole = buffer.at[pl.ds(0, zs - 1), items]
+        pltpu.make_async_copy(whole, whole, sems.at[0, group]).wait()
 
     def spread_z(phase, item, source, target):
-        @pl.loop(1, zs)
-        def _(step):
+        for step in z_order(zs):
             peer = z_peer(step)
             pltpu.make_async_remote_copy(
                 src_ref=source.at[item, peer],
@@ -145,8 +171,7 @@
             ).start()
 
     def spread_b(phase, item, source, target):
-        @pl.loop(1, bs)
-        def _(step):
+        for step in b_order(bs):
             peer = b_peer(step)
             pltpu.make_async_remote_copy(
                 src_ref=source.at[item, peer],
@@ -161,6 +186,7 @@
         whole = buffer.at[item, pl.ds(0, count - 1)]
         pltpu.make_async_copy(whole, whole, sems.at[phase, item]).wait()
 
+    groups = (pl.ds(0, 2), pl.ds(2, 1))
     loads[0].wait()
     loads[1].wait()
     fill(0, k_ref[...] * v_ref[...])
@@ -170,8 +196,8 @@
     loads[4].wait()
     fill(2, o_ref[...] * q_ref[...])
     pl.semaphore_wait(barrier, zs - 1 + bs - 1)
-    for item in range(ITEMS):
-        spread_z(0, item, a_send, a_recv)
+    for group, items in enumerate(groups):
+        spread_a(group, items)
     for load in loads[5:]:
         load.wait()
     first = (table_refs[0], table_refs[1])
@@ -184,8 +210,7 @@
         return refs[0][...], refs[1][...]
 
     def forward(item):
-        await_all(recv_sem, 0, item, a_recv, zs)
-        rows = a_recv[item].reshape(run, LANES)
+        rows = a_recv[:, item].reshape(run, LANES)
         sums = dot3(pair(first), split(rows))
         real, imag = sums[:run], sums[run:]
         cos, sin = turn_real[...], turn_imag[...]
@@ -252,8 +277,10 @@
         d_recv[item, lane] = d_send[item, lane]
         spread_z(3, item, d_send, d_recv)
 
+    await_a(recv_sem, 0, groups[0], a_recv)
     forward(0)
     forward(1)
+    await_a(recv_sem, 1, groups[1], a_recv)
     forward(2)
     await_all(recv_sem, 1, 0, b_recv, bs)
     await_all(recv_sem, 1, 1, b_recv, bs)
@@ -265,27 +292,41 @@
     inverse(1)
     inverse(2)
 
+    stores = []
+
+    def store(item, at, count):
+        rows = pl.ds(at, count)
+        copy = pltpu.make_async_copy(out_ref.at[rows], out_hbm.at[rows], out_sem.at[item])
+        copy.start()
+        stores.append(copy)
+
     for item in range(ITEMS):
-        await_all(send_sem, 0, item, a_send, zs)
         await_all(send_sem, 1, item, b_send, bs)
         await_all(send_sem, 2, item, c_send, bs)
+    for group, items in enumerate(groups):
+        await_a(send_sem, group, items, a_send)
     await_all(recv_sem, 3, 0, d_recv, zs)
     for row in range(ROWS):
         here = slice(row * LANES, (row + 1) * LANES)
         mixed = d_recv[0, :, row, :]
-        out_refs[0][:, here] = q_ref[:, here] * mixed
-        out_refs[1][:, here] = o_ref[:, here] * mixed
+        out_ref[0, :, here] = q_ref[:, here] * mixed
+        out_ref[1, :, here] = o_ref[:, here] * mixed
+    store(0, 0, 2)
     await_all(recv_sem, 3, 1, d_recv, zs)
     for row in range(ROWS):
         here = slice(row * LANES, (row + 1) * LANES)
         gated_grad = d_recv[1, :, row, :]
-        out_refs[2][:, here] = gated_grad * v_ref[:, here]
-        out_refs[3][:, here] = gated_grad * k_ref[:, here]
+        out_ref[2, :, here] = gated_grad * v_ref[:, here]
+        out_ref[3, :, here] = gated_grad * k_ref[:, here]
+    store(1, 2, 2)
     await_all(recv_sem, 3, 2, d_recv, zs)
     for row in range(ROWS):
-        out_refs[4][:, row * LANES : (row + 1) * LANES] = d_recv[2, :, row, :]
+        out_ref[4, :, row * LANES : (row + 1) * LANES] = d_recv[2, :, row, :]
+    store(2, 4, 1)
     for item in range(ITEMS):
         await_all(send_sem, 3, item, d_send, zs)
+    for copy in stores:
+        copy.wait()
 
 
 def per_device(query_proj, key_proj, value_proj, filter_taps, out_cotangent):
@@ -297,32 +338,34 @@
     part = run // bs
     scale = 1.0 / (run * LANES * math.sqrt(tokens * devices))
     table = tables(run)
-    shape = jax.ShapeDtypeStruct((channels, tokens), jnp.float32)
+    a_buffer = pltpu.VMEM((zs, ITEMS, ROWS, LANES), jnp.float32)
     z_buffer = pltpu.VMEM((ITEMS, zs, ROWS, LANES), jnp.float32)
     b_buffer = pltpu.VMEM((ITEMS, bs, 2, part, LANES), jnp.float32)
     body = lambda *refs: kernel(zs, bs, scale, *refs)
     outs = pl.pallas_call(
         body,
-        out_shape=[shape] * 5,
+        out_shape=jax.ShapeDtypeStruct((5, channels, tokens), jnp.float32),
         in_specs=[pl.BlockSpec(memory_space=pl.ANY)] * (5 + len(table)),
-        out_specs=[pl.BlockSpec(memory_space=pltpu.VMEM)] * 5,
+        out_specs=pl.BlockSpec(memory_space=pl.ANY),
         scratch_shapes=[
             *[pltpu.VMEM((channels, tokens), jnp.float32) for _ in range(5)],
             *[pltpu.VMEM(entry.shape, entry.dtype) for entry in table],
-            z_buffer,
-            z_buffer,
+            a_buffer,
+            a_buffer,
             b_buffer,
             b_buffer,
             b_buffer,
             b_buffer,
             z_buffer,
             z_buffer,
+            pltpu.VMEM((5, channels, tokens), jnp.float32),
             pltpu.SemaphoreType.DMA((5 + len(table),)),
+            pltpu.SemaphoreType.DMA((3,)),
             pltpu.SemaphoreType.DMA((4, ITEMS)),
             pltpu.SemaphoreType.DMA((4, ITEMS)),
         ],
         compiler_params=pltpu.CompilerParams(
-            collective_id=0, has_side_effects=True, vmem_limit_bytes=32 * 1024 * 1024
+            collective_id=0, has_side_effects=True, vmem_limit_bytes=60 * 1024 * 1024
         ),
     )(
         query_proj,
@@ -332,7 +375,7 @@
         out_cotangent,
         *[jnp.asarray(entry) for entry in table],
     )
-    return tuple(outs)
+    return tuple(outs[at] for at in range(5))
 
 
 def solution(mesh):

time: 67.1 us -> 49.8 us (0.74)
  the two profiles are of different devices: /device:TPU:2 before, /device:TPU:6 now
where the time goes in v1:
time: 49.8 us; the launch traced here: 49.2 us
  Pallas kernels  46.8 us (94%)
  local copies, waits for them, and re-layouts  1.69 us (3%)
  between operations  0.64 us (1%)
    pallas_call x1, Pallas kernels, per_device(): pl.pallas_call(body, out_shape=jax.ShapeDtypeStruct((5, channels, tokens)...  46.8 us
    squeeze x1, local copies, waits for them, and re-layouts, per_device(): return tuple((outs[at] for at in range(5)))  1.69 us

profile of v1, /device:TPU:6, one launch (start us, length us, event | category | flops | bytes accessed | tf_op | source)
XLA Modules:
  0.0 49.2 jit_solution(13275426374611509486)
XLA Ops:
  0.6 46.8 %shard_map.182 = f32[5,16,1024]{2,1,0:T(8,128)} custom-call(f32[16,1024]{1,0:T(8,128)} %refs_0_.1, f32[16,1024]{1,0:T(8,128)} %refs_1_.1, f32[16,1024]{1,0:T(8,128)} %refs_2_.1, f32[16,1024]{1,0:T(8,128)} %refs_3_.1, f32[16,1024]{1,0:T(8,128)} %refs_4_.1, bf16[256,128]{1,0:T(8,128)(2,1)} %constant.20.clone.refs_5_, bf16[256,128]{1,0:T(8,128)(2,1)} %constant.21.clone.refs_6_, ...), custom_call_target="tpu_custom_call" | custom-call | tf_op jit(solution)/shard_map/pallas_call | solution.py:345
  47.5 1.7 %slice_bitcast_fusion = (f32[16,1024]{1,0:T(8,128)}, f32[16,1024]{1,0:T(8,128)}, f32[16,1024]{1,0:T(8,128)}, f32[16,1024]{1,0:T(8,128)}, f32[16,1024]{1,0:T(8,128)}) fusion(f32[5,16,1024]{2,1,0:T(8,128)} %shard_map.182), kind=kLoop, calls=%fused_computation | loop fusion | bytes 655360 | tf_op jit(solution)/shard_map/squeeze | solution.py:378

commit v2 on v1

v2 whole, which is shorter than its diff:
```python
import math

import jax
import jax.numpy as jnp
import numpy as np
from jax import lax
from jax.experimental import pallas as pl
from jax.experimental.pallas import tpu as pltpu
from jax.sharding import PartitionSpec as P

MESH = pl.DeviceIdType.MESH
LANES = 128
ROWS = 8
ITEMS = 3


def split_np(matrix):
    high = matrix.astype(jnp.bfloat16)
    low = (matrix - high.astype(np.float64)).astype(jnp.bfloat16)
    return high, low


def tables(run):
    k1 = np.arange(run)[:, None]
    n1 = np.arange(run)[None, :]
    first = ((2 * k1 + 1) * n1 % (4 * run)) * (2.0 * math.pi / (4 * run))
    first = np.concatenate([np.cos(first), -np.sin(first)], axis=0)
    n2 = np.arange(LANES)[None, :]
    turn = ((2 * k1 + 1) * n2) * (2.0 * math.pi / (4 * run * LANES))
    square = (np.arange(LANES)[:, None] * n2 % LANES) * (2.0 * math.pi / LANES)
    cos, sin = np.cos(square), np.sin(square)
    second = np.block([[cos, -sin], [sin, cos]])
    def left(matrix):
        high, low = split_np(matrix)
        return np.concatenate([high, high, low], axis=1)

    def right(matrix):
        high, low = split_np(matrix)
        return np.concatenate([high, high, low], axis=0)

    return (
        left(first),
        np.cos(turn).astype(np.float32),
        (-np.sin(turn)).astype(np.float32),
        right(second),
        right(second.T),
        left(first.T),
    )


def split(value):
    high = value.astype(jnp.bfloat16)
    low = (value - high.astype(jnp.float32)).astype(jnp.bfloat16)
    return high, low


def dot(left, right):
    return jnp.dot(left, right, preferred_element_type=jnp.float32)


def dot_left(table, value):
    high, low = split(value)
    return dot(table, jnp.concatenate([high, low, high], axis=0))


def dot_right(value, table):
    high, low = split(value)
    return dot(jnp.concatenate([high, low, high], axis=1), table)


def z_order(count):
    near = [step for half in range((count - 1) // 2, 0, -1) for step in (half, count - half)]
    return ([count // 2] if count % 2 == 0 else []) + near


def b_order(count):
    wide = count // 2
    steps = [(dx, dy) for dx in range(2) for dy in range(wide) if dx or dy]
    return sorted(steps, key=lambda step: -(step[0] + min(step[1], wide - step[1])))


def kernel(
    zs,
    bs,
    scale,
    q_hbm,
    k_hbm,
    v_hbm,
    f_hbm,
    o_hbm,
    *rest,
):
    table_hbm = rest[:6]
    out_ref = rest[6]
    (
        q_ref,
        k_ref,
        v_ref,
        f_ref,
        o_ref,
        *table_refs,
    ) = rest[7:18]
    (
        a_send,
        a_recv,
        b_send,
        b_recv,
        c_send,
        c_recv,
        d_send,
        d_recv,
        in_sem,
        send_sem,
        recv_sem,
    ) = rest[18:]
    run = zs * ROWS
    part = run // bs
    me = lax.axis_index("seq")
    block = me // zs
    lane = me % zs

    def z_peer(step):
        return lax.rem(lane + step, zs)

    def b_peer(step):
        wide = bs // 2
        across = lax.rem(lax.div(block, wide) + step[0], 2)
        return across * wide + lax.rem(lax.rem(block, wide) + step[1], wide)

    barrier = pltpu.get_barrier_semaphore()
    for step in z_order(zs):
        pl.semaphore_signal(
            barrier, inc=1, device_id={"seq": block * zs + z_peer(step)}, device_id_type=MESH
        )
    for step in b_order(bs):
        pl.semaphore_signal(
            barrier, inc=1, device_id={"seq": b_peer(step) * zs + lane}, device_id_type=MESH
        )

    loads = [
        pltpu.make_async_copy(src, dst, in_sem.at[at])
        for at, (src, dst) in enumerate(
            zip(
                (k_hbm, v_hbm, f_hbm, o_hbm, q_hbm) + tuple(table_hbm),
                (k_ref, v_ref, f_ref, o_ref, q_ref) + tuple(table_refs),
            )
        )
    ]
    for load in loads:
        load.start()

    def fill(item, value):
        for row in range(ROWS):
            a_send[:, item, row, :] = value[:, row * LANES : (row + 1) * LANES]
        a_recv[lane, item] = a_send[lane, item]

    def spread_z(phase, group, items, source, target):
        for step in z_order(zs):
            peer = z_peer(step)
            pltpu.make_async_remote_copy(
                src_ref=source.at[peer, items],
                dst_ref=target.at[lane, items],
                send_sem=send_sem.at[phase, group],
                recv_sem=recv_sem.at[phase, group],
                device_id={"seq": block * zs + peer},
                device_id_type=MESH,
            ).start()

    def await_z(sems, phase, group, items, buffer):
        whole = buffer.at[pl.ds(0, zs - 1), items]
        pltpu.make_async_copy(whole, whole, sems.at[phase, group]).wait()

    def spread_b(phase, item, source, target):
        for step in b_order(bs):
            peer = b_peer(step)
            pltpu.make_async_remote_copy(
                src_ref=source.at[item, peer],
                dst_ref=target.at[item, block],
                send_sem=send_sem.at[phase, item],
                recv_sem=recv_sem.at[phase, item],
                device_id={"seq": peer * zs + lane},
                device_id_type=MESH,
            ).start()

    def spread_c(group, items):
        for step in b_order(bs):
            peer = b_peer(step)
            pltpu.make_async_remote_copy(
                src_ref=c_send.at[peer, items],
                dst_ref=c_recv.at[block, items],
                send_sem=send_sem.at[2, group],
                recv_sem=recv_sem.at[2, group],
                device_id={"seq": peer * zs + lane},
                device_id_type=MESH,
            ).start()

    def await_c(sems, group, items, buffer):
        whole = buffer.at[pl.ds(0, bs - 1), items]
        pltpu.make_async_copy(whole, whole, sems.at[2, group]).wait()

    def await_all(sems, phase, item, buffer, count):
        whole = buffer.at[item, pl.ds(0, count - 1)]
        pltpu.make_async_copy(whole, whole, sems.at[phase, item]).wait()

    groups = (pl.ds(0, 2), pl.ds(2, 1))
    returns = (pl.ds(0, 1), pl.ds(1, 2))
    loads[0].wait()
    loads[1].wait()
    fill(0, k_ref[...] * v_ref[...])
    loads[2].wait()
    fill(1, f_ref[...])
    loads[3].wait()
    loads[4].wait()
    fill(2, o_ref[...] * q_ref[...])
    pl.semaphore_wait(barrier, zs - 1 + bs - 1)
    for group, items in enumerate(groups):
        spread_z(0, group, items, a_send, a_recv)
    for load in loads[5:]:
        load.wait()
    first, turn_real, turn_imag, second, second_back, first_back = table_refs

    def forward(items):
        rows = [a_recv[:, item].reshape(run, LANES) for item in items]
        sums = dot_left(first[...], jnp.concatenate(rows, axis=1))
        cos, sin = turn_real[...], turn_imag[...]
        turned = []
        for at in range(len(items)):
            here = slice(at * LANES, (at + 1) * LANES)
            real, imag = sums[:run, here], sums[run:, here]
            turned.append(
                jnp.concatenate([real * cos - imag * sin, real * sin + imag * cos], axis=1)
            )
        bins = dot_right(jnp.concatenate(turned, axis=0), second[...])
        for at, item in enumerate(items):
            here = slice(at * run, (at + 1) * run)
            b_send[item, :, 0] = bins[here, :LANES].reshape(bs, part, LANES)
            b_send[item, :, 1] = bins[here, LANES:].reshape(bs, part, LANES)
            b_recv[item, block] = b_send[item, block]
            spread_b(1, item, b_send, b_recv)

    sign = 1.0 - 2.0 * (lax.broadcasted_iota(jnp.int32, (part, LANES), 0) % 2).astype(jnp.float32)

    def spectrum(item, at):
        return b_recv[item, at, 0], b_recv[item, at, 1]

    def finish(item, sums, step, factor):
        for at in range(bs):
            real, imag = sums[at]
            other = at + step
            if 0 <= other < bs:
                over_real, over_imag = sums[other]
                real = real - factor * over_imag
                imag = imag + factor * over_real
            c_send[at, item, 0] = real
            c_send[at, item, 1] = imag
        c_recv[block, item] = c_send[block, item]

    def convolve(item, left, right):
        sums = []
        for at in range(bs):
            real = imag = None
            for of in range(at + 1):
                lr, li = spectrum(left, at - of)
                rr, ri = spectrum(right, of)
                pr, pi = lr * rr - li * ri, lr * ri + li * rr
                real, imag = (pr, pi) if real is None else (real + pr, imag + pi)
            sums.append((real, imag))
        finish(item, sums, -1, sign)

    def correlate(item, left, right):
        sums = []
        for at in range(bs):
            real = imag = None
            for of in range(bs - at):
                lr, li = spectrum(left, of)
                rr, ri = spectrum(right, at + of)
                pr, pi = lr * rr + li * ri, lr * ri - li * rr
                real, imag = (pr, pi) if real is None else (real + pr, imag + pi)
            sums.append((real, imag))
        finish(item, sums, 1, -sign)

    def inverse(items):
        bins = [
            jnp.concatenate(
                [c_recv[:, item, half].reshape(run, LANES) for half in range(2)], axis=1
            )
            for item in items
        ]
        sums = dot_right(jnp.concatenate(bins, axis=0), second_back[...])
        cos, sin = turn_real[...], turn_imag[...]
        turned = []
        for at in range(len(items)):
            here = slice(at * run, (at + 1) * run)
            real, imag = sums[here, :LANES], sums[here, LANES:]
            turned.append(
                jnp.concatenate([real * cos + imag * sin, imag * cos - real * sin], axis=0)
            )
        rows = dot_left(first_back[...], jnp.concatenate(turned, axis=1)) * scale
        for at, item in enumerate(items):
            here = slice(at * LANES, (at + 1) * LANES)
            d_send[:, item] = rows[:, here].reshape(zs, ROWS, LANES)
            d_recv[lane, item] = d_send[lane, item]

    await_z(recv_sem, 0, 0, groups[0], a_recv)
    forward((0, 1))
    await_z(recv_sem, 0, 1, groups[1], a_recv)
    forward((2,))
    await_all(recv_sem, 1, 0, b_recv, bs)
    await_all(recv_sem, 1, 1, b_recv, bs)
    convolve(0, 1, 0)
    spread_c(0, returns[0])
    await_all(recv_sem, 1, 2, b_recv, bs)
    correlate(1, 1, 2)
    correlate(2, 0, 2)
    spread_c(1, returns[1])
    await_c(recv_sem, 0, returns[0], c_recv)
    inverse((0,))
    spread_z(3, 0, returns[0], d_send, d_recv)
    await_c(recv_sem, 1, returns[1], c_recv)
    inverse((1, 2))
    spread_z(3, 1, returns[1], d_send, d_recv)

    for item in range(ITEMS):
        await_all(send_sem, 1, item, b_send, bs)
    for group, items in enumerate(returns):
        await_c(send_sem, group, items, c_send)
    for group, items in enumerate(groups):
        await_z(send_sem, 0, group, items, a_send)
    await_z(recv_sem, 3, 0, returns[0], d_recv)
    for row in range(ROWS):
        here = slice(row * LANES, (row + 1) * LANES)
        mixed = d_recv[:, 0, row, :]
        out_ref[0, :, here] = q_ref[:, here] * mixed
        out_ref[1, :, here] = o_ref[:, here] * mixed
    await_z(recv_sem, 3, 1, returns[1], d_recv)
    for row in range(ROWS):
        here = slice(row * LANES, (row + 1) * LANES)
        gated_grad = d_recv[:, 1, row, :]
        out_ref[2, :, here] = gated_grad * v_ref[:, here]
        out_ref[3, :, here] = gated_grad * k_ref[:, here]
    for row in range(ROWS):
        out_ref[4, :, row * LANES : (row + 1) * LANES] = d_recv[:, 2, row, :]
    for group, items in enumerate(returns):
        await_z(send_sem, 3, group, items, d_send)


def per_device(query_proj, key_proj, value_proj, filter_taps, out_cotangent):
    devices = lax.axis_size("seq")
    channels, tokens = filter_taps.shape
    zs = channels
    bs = devices // zs
    run = zs * ROWS
    part = run // bs
    scale = 1.0 / (run * LANES * math.sqrt(tokens * devices))
    table = tables(run)
    z_buffer = pltpu.VMEM((zs, ITEMS, ROWS, LANES), jnp.float32)
    c_buffer = pltpu.VMEM((bs, ITEMS, 2, part, LANES), jnp.float32)
    b_buffer = pltpu.VMEM((ITEMS, bs, 2, part, LANES), jnp.float32)
    body = lambda *refs: kernel(zs, bs, scale, *refs)
    outs = pl.pallas_call(
        body,
        out_shape=pltpu.VMEM((5, channels, tokens), jnp.float32),
        in_specs=[pl.BlockSpec(memory_space=pl.ANY)] * (5 + len(table)),
        out_specs=pl.BlockSpec(memory_space=pltpu.VMEM),
        scratch_shapes=[
            *[pltpu.VMEM((channels, tokens), jnp.float32) for _ in range(5)],
            *[pltpu.VMEM(entry.shape, entry.dtype) for entry in table],
            z_buffer,
            z_buffer,
            b_buffer,
            b_buffer,
            c_buffer,
            c_buffer,
            z_buffer,
            z_buffer,
            pltpu.SemaphoreType.DMA((5 + len(table),)),
            pltpu.SemaphoreType.DMA((4, ITEMS)),
            pltpu.SemaphoreType.DMA((4, ITEMS)),
        ],
        compiler_params=pltpu.CompilerParams(
            collective_id=0, has_side_effects=True, vmem_limit_bytes=60 * 1024 * 1024
        ),
    )(
        query_proj,
        key_proj,
        value_proj,
        filter_taps,
        out_cotangent,
        *[jnp.asarray(entry) for entry in table],
    )
    return tuple(outs[at] for at in range(5))


def solution(mesh):
    placed = (P("ch", "seq"),) * 5
    return jax.shard_map(
        per_device, mesh=mesh, in_specs=placed, out_specs=placed, check_vma=False
    )
```

time: 49.8 us -> 47.7 us (0.958)
  local copies, waits for them, and re-layouts: 1.69 us -> 0.72 us
  Pallas kernels: 46.8 us -> 46.2 us
    squeeze x1, local copies, waits for them, and re-layouts: 1.69 us -> 0.72 us  [per_device(): return tuple((outs[at] for at in range(5)))]
    pallas_call x1, Pallas kernels: 46.8 us -> 46.2 us  [per_device(): pl.pallas_call(body, out_shape=pltpu.VMEM((5, channels, tokens), jnp.floa...]
where the time goes in v2:
time: 47.7 us; the launch traced here: 47.6 us
  Pallas kernels  46.2 us (97%)
  local copies, waits for them, and re-layouts  0.72 us (2%)
  between operations  0.64 us (1%)
    pallas_call x1, Pallas kernels, per_device(): pl.pallas_call(body, out_shape=pltpu.VMEM((5, channels, tokens), jnp.floa...  46.2 us

profile of v2, /device:TPU:6, one launch (start us, length us, event | category | flops | bytes accessed | tf_op | source)
XLA Modules:
  0.0 47.6 jit_solution(4834865687923175308)
XLA Ops:
  0.6 46.2 %shard_map.146 = f32[5,16,1024]{2,1,0:T(8,128)S(1)} custom-call(f32[16,1024]{1,0:T(8,128)} %refs_0_.1, f32[16,1024]{1,0:T(8,128)} %refs_1_.1, f32[16,1024]{1,0:T(8,128)} %refs_2_.1, f32[16,1024]{1,0:T(8,128)} %refs_3_.1, f32[16,1024]{1,0:T(8,128)} %refs_4_.1, bf16[256,384]{1,0:T(8,128)(2,1)} %constant.12.clone.refs_5_, f32[128,128]{1,0:T(8,128)} %constant.13.clone.refs_6_, ...), custom_call_target="tpu_custom_call" | custom-call | tf_op jit(solution)/shard_map/pallas_call | solution.py:360
  46.8 0.7 %slice_bitcast_fusion = (f32[16,1024]{1,0:T(8,128)}, f32[16,1024]{1,0:T(8,128)}, f32[16,1024]{1,0:T(8,128)}, f32[16,1024]{1,0:T(8,128)}, f32[16,1024]{1,0:T(8,128)}) fusion(f32[5,16,1024]{2,1,0:T(8,128)S(1)} %shard_map.146), kind=kLoop, calls=%fused_computation | loop fusion | bytes 655360 | tf_op jit(solution)/shard_map/squeeze | solution.py:391

commit v3 on v2

--- a/solution.py
+++ b/solution.py
@@ -204,6 +204,7 @@
 
     groups = (pl.ds(0, 2), pl.ds(2, 1))
     returns = (pl.ds(0, 1), pl.ds(1, 2))
+    thirds = (pl.ds(0, 1), pl.ds(1, 1), pl.ds(2, 1))
     loads[0].wait()
     loads[1].wait()
     fill(0, k_ref[...] * v_ref[...])
@@ -311,18 +312,20 @@
     spread_c(0, returns[0])
     await_all(recv_sem, 1, 2, b_recv, bs)
     correlate(1, 1, 2)
+    spread_c(1, thirds[1])
     correlate(2, 0, 2)
-    spread_c(1, returns[1])
+    spread_c(2, thirds[2])
     await_c(recv_sem, 0, returns[0], c_recv)
     inverse((0,))
     spread_z(3, 0, returns[0], d_send, d_recv)
-    await_c(recv_sem, 1, returns[1], c_recv)
+    await_c(recv_sem, 1, thirds[1], c_recv)
+    await_c(recv_sem, 2, thirds[2], c_recv)
     inverse((1, 2))
     spread_z(3, 1, returns[1], d_send, d_recv)
 
     for item in range(ITEMS):
         await_all(send_sem, 1, item, b_send, bs)
-    for group, items in enumerate(returns):
+    for group, items in enumerate(thirds):
         await_c(send_sem, group, items, c_send)
     for group, items in enumerate(groups):
         await_z(send_sem, 0, group, items, a_send)

time: 47.7 us -> 47.7 us (level)
  no operation moved by 1% of the time
where the time goes in v3:
time: 47.7 us; the launch traced here: 47.6 us
  Pallas kernels  46.2 us (97%)
  local copies, waits for them, and re-layouts  0.72 us (2%)
  between operations  0.64 us (1%)
    pallas_call x1, Pallas kernels, per_device(): pl.pallas_call(body, out_shape=pltpu.VMEM((5, channels, tokens), jnp.floa...  46.2 us

profile of v3, /device:TPU:6, one launch (start us, length us, event | category | flops | bytes accessed | tf_op | source)
XLA Modules:
  0.0 47.6 jit_solution(14821918070352518261)
XLA Ops:
  0.6 46.2 %shard_map.146 = f32[5,16,1024]{2,1,0:T(8,128)S(1)} custom-call(f32[16,1024]{1,0:T(8,128)} %refs_0_.1, f32[16,1024]{1,0:T(8,128)} %refs_1_.1, f32[16,1024]{1,0:T(8,128)} %refs_2_.1, f32[16,1024]{1,0:T(8,128)} %refs_3_.1, f32[16,1024]{1,0:T(8,128)} %refs_4_.1, bf16[256,384]{1,0:T(8,128)(2,1)} %constant.12.clone.refs_5_, f32[128,128]{1,0:T(8,128)} %constant.13.clone.refs_6_, ...), custom_call_target="tpu_custom_call" | custom-call | tf_op jit(solution)/shard_map/pallas_call | solution.py:363
  46.9 0.7 %slice_bitcast_fusion = (f32[16,1024]{1,0:T(8,128)}, f32[16,1024]{1,0:T(8,128)}, f32[16,1024]{1,0:T(8,128)}, f32[16,1024]{1,0:T(8,128)}, f32[16,1024]{1,0:T(8,128)}) fusion(f32[5,16,1024]{2,1,0:T(8,128)S(1)} %shard_map.146), kind=kLoop, calls=%fused_computation | loop fusion | bytes 655360 | tf_op jit(solution)/shard_map/squeeze | solution.py:394

commit v4 on v3

--- a/solution.py
+++ b/solution.py
@@ -155,8 +155,8 @@
         a_recv[lane, item] = a_send[lane, item]
 
     def spread_z(phase, group, items, source, target):
-        for step in z_order(zs):
-            peer = z_peer(step)
+        for at, step in enumerate(z_order(zs)):
+            peer = at + (lane <= at).astype(jnp.int32) if phase == 3 else z_peer(step)
             pltpu.make_async_remote_copy(
                 src_ref=source.at[peer, items],
                 dst_ref=target.at[lane, items],

time: 47.7 us -> 47.3 us (level)
  Pallas kernels: 46.2 us -> 45.5 us
    pallas_call x1, Pallas kernels: 46.2 us -> 45.5 us  [per_device(): pl.pallas_call(body, out_shape=pltpu.VMEM((5, channels, tokens), jnp.floa...]
where the time goes in v4:
time: 47.3 us; the launch traced here: 46.9 us
  Pallas kernels  45.5 us (96%)
  local copies, waits for them, and re-layouts  0.72 us (2%)
  between operations  0.64 us (1%)
    pallas_call x1, Pallas kernels, per_device(): pl.pallas_call(body, out_shape=pltpu.VMEM((5, channels, tokens), jnp.floa...  45.5 us

profile of v4, /device:TPU:6, one launch (start us, length us, event | category | flops | bytes accessed | tf_op | source)
XLA Modules:
  0.0 46.9 jit_solution(12528397338547547674)
XLA Ops:
  0.6 45.5 %shard_map.146 = f32[5,16,1024]{2,1,0:T(8,128)S(1)} custom-call(f32[16,1024]{1,0:T(8,128)} %refs_0_.1, f32[16,1024]{1,0:T(8,128)} %refs_1_.1, f32[16,1024]{1,0:T(8,128)} %refs_2_.1, f32[16,1024]{1,0:T(8,128)} %refs_3_.1, f32[16,1024]{1,0:T(8,128)} %refs_4_.1, bf16[256,384]{1,0:T(8,128)(2,1)} %constant.12.clone.refs_5_, f32[128,128]{1,0:T(8,128)} %constant.13.clone.refs_6_, ...), custom_call_target="tpu_custom_call" | custom-call | tf_op jit(solution)/shard_map/pallas_call | solution.py:363
  46.1 0.7 %slice_bitcast_fusion = (f32[16,1024]{1,0:T(8,128)}, f32[16,1024]{1,0:T(8,128)}, f32[16,1024]{1,0:T(8,128)}, f32[16,1024]{1,0:T(8,128)}, f32[16,1024]{1,0:T(8,128)}) fusion(f32[5,16,1024]{2,1,0:T(8,128)S(1)} %shard_map.146), kind=kLoop, calls=%fused_computation | loop fusion | bytes 655360 | tf_op jit(solution)/shard_map/squeeze | solution.py:394

commit v5 on v4

--- a/solution.py
+++ b/solution.py
@@ -170,37 +170,21 @@
         whole = buffer.at[pl.ds(0, zs - 1), items]
         pltpu.make_async_copy(whole, whole, sems.at[phase, group]).wait()
 
-    def spread_b(phase, item, source, target):
+    def spread_b(phase, group, items, source, target):
         for step in b_order(bs):
             peer = b_peer(step)
             pltpu.make_async_remote_copy(
-                src_ref=source.at[item, peer],
-                dst_ref=target.at[item, block],
-                send_sem=send_sem.at[phase, item],
-                recv_sem=recv_sem.at[phase, item],
+                src_ref=source.at[peer, items],
+                dst_ref=target.at[block, items],
+                send_sem=send_sem.at[phase, group],
+                recv_sem=recv_sem.at[phase, group],
                 device_id={"seq": peer * zs + lane},
                 device_id_type=MESH,
             ).start()
 
-    def spread_c(group, items):
-        for step in b_order(bs):
-            peer = b_peer(step)
-            pltpu.make_async_remote_copy(
-                src_ref=c_send.at[peer, items],
-                dst_ref=c_recv.at[block, items],
-                send_sem=send_sem.at[2, group],
-                recv_sem=recv_sem.at[2, group],
-                device_id={"seq": peer * zs + lane},
-                device_id_type=MESH,
-            ).start()
-
-    def await_c(sems, group, items, buffer):
+    def await_b(sems, phase, group, items, buffer):
         whole = buffer.at[pl.ds(0, bs - 1), items]
-        pltpu.make_async_copy(whole, whole, sems.at[2, group]).wait()
-
-    def await_all(sems, phase, item, buffer, count):
-        whole = buffer.at[item, pl.ds(0, count - 1)]
-        pltpu.make_async_copy(whole, whole, sems.at[phase, item]).wait()
+        pltpu.make_async_copy(whole, whole, sems.at[phase, group]).wait()
 
     groups = (pl.ds(0, 2), pl.ds(2, 1))
     returns = (pl.ds(0, 1), pl.ds(1, 2))
@@ -234,15 +218,14 @@
         bins = dot_right(jnp.concatenate(turned, axis=0), second[...])
         for at, item in enumerate(items):
             here = slice(at * run, (at + 1) * run)
-            b_send[item, :, 0] = bins[here, :LANES].reshape(bs, part, LANES)
-            b_send[item, :, 1] = bins[here, LANES:].reshape(bs, part, LANES)
-            b_recv[item, block] = b_send[item, block]
-            spread_b(1, item, b_send, b_recv)
+            b_send[:, item, 0] = bins[here, :LANES].reshape(bs, part, LANES)
+            b_send[:, item, 1] = bins[here, LANES:].reshape(bs, part, LANES)
+            b_recv[block, item] = b_send[block, item]
 
     sign = 1.0 - 2.0 * (lax.broadcasted_iota(jnp.int32, (part, LANES), 0) % 2).astype(jnp.float32)
 
     def spectrum(item, at):
-        return b_recv[item, at, 0], b_recv[item, at, 1]
+        return b_recv[at, item, 0], b_recv[at, item, 1]
 
     def finish(item, sums, step, factor):
         for at in range(bs):
@@ -304,29 +287,30 @@
 
     await_z(recv_sem, 0, 0, groups[0], a_recv)
     forward((0, 1))
+    spread_b(1, 0, groups[0], b_send, b_recv)
     await_z(recv_sem, 0, 1, groups[1], a_recv)
     forward((2,))
-    await_all(recv_sem, 1, 0, b_recv, bs)
-    await_all(recv_sem, 1, 1, b_recv, bs)
+    spread_b(1, 1, groups[1], b_send, b_recv)
+    await_b(recv_sem, 1, 0, groups[0], b_recv)
     convolve(0, 1, 0)
-    spread_c(0, returns[0])
-    await_all(recv_sem, 1, 2, b_recv, bs)
+    spread_b(2, 0, returns[0], c_send, c_recv)
+    await_b(recv_sem, 1, 1, groups[1], b_recv)
     correlate(1, 1, 2)
-    spread_c(1, thirds[1])
+    spread_b(2, 1, thirds[1], c_send, c_recv)
     correlate(2, 0, 2)
-    spread_c(2, thirds[2])
-    await_c(recv_sem, 0, returns[0], c_recv)
+    spread_b(2, 2, thirds[2], c_send, c_recv)
+    await_b(recv_sem, 2, 0, returns[0], c_recv)
     inverse((0,))
     spread_z(3, 0, returns[0], d_send, d_recv)
-    await_c(recv_sem, 1, thirds[1], c_recv)
-    await_c(recv_sem, 2, thirds[2], c_recv)
+    await_b(recv_sem, 2, 1, thirds[1], c_recv)
+    await_b(recv_sem, 2, 2, thirds[2], c_recv)
     inverse((1, 2))
     spread_z(3, 1, returns[1], d_send, d_recv)
 
-    for item in range(ITEMS):
-        await_all(send_sem, 1, item, b_send, bs)
+    for group, items in enumerate(groups):
+        await_b(send_sem, 1, group, items, b_send)
     for group, items in enumerate(thirds):
-        await_c(send_sem, group, items, c_send)
+        await_b(send_sem, 2, group, items, c_send)
     for group, items in enumerate(groups):
         await_z(send_sem, 0, group, items, a_send)
     await_z(recv_sem, 3, 0, returns[0], d_recv)
@@ -357,8 +341,7 @@
     scale = 1.0 / (run * LANES * math.sqrt(tokens * devices))
     table = tables(run)
     z_buffer = pltpu.VMEM((zs, ITEMS, ROWS, LANES), jnp.float32)
-    c_buffer = pltpu.VMEM((bs, ITEMS, 2, part, LANES), jnp.float32)
-    b_buffer = pltpu.VMEM((ITEMS, bs, 2, part, LANES), jnp.float32)
+    b_buffer = pltpu.VMEM((bs, ITEMS, 2, part, LANES), jnp.float32)
     body = lambda *refs: kernel(zs, bs, scale, *refs)
     outs = pl.pallas_call(
         body,
@@ -372,8 +355,8 @@
             z_buffer,
             b_buffer,
             b_buffer,
-            c_buffer,
-            c_buffer,
+            b_buffer,
+            b_buffer,
             z_buffer,
             z_buffer,
             pltpu.SemaphoreType.DMA((5 + len(table),)),

time: 47.3 us -> 47.4 us (level)
  no operation moved by 1% of the time
where the time goes in v5:
time: 47.4 us; the launch traced here: 46.9 us
  Pallas kernels  45.6 us (96%)
  local copies, waits for them, and re-layouts  0.72 us (2%)
  between operations  0.64 us (1%)
    pallas_call x1, Pallas kernels, per_device(): pl.pallas_call(body, out_shape=pltpu.VMEM((5, channels, tokens), jnp.floa...  45.6 us

profile of v5, /device:TPU:6, one launch (start us, length us, event | category | flops | bytes accessed | tf_op | source)
XLA Modules:
  0.0 46.9 jit_solution(5572913162440895055)
XLA Ops:
  0.6 45.6 %shard_map.146 = f32[5,16,1024]{2,1,0:T(8,128)S(1)} custom-call(f32[16,1024]{1,0:T(8,128)} %refs_0_.1, f32[16,1024]{1,0:T(8,128)} %refs_1_.1, f32[16,1024]{1,0:T(8,128)} %refs_2_.1, f32[16,1024]{1,0:T(8,128)} %refs_3_.1, f32[16,1024]{1,0:T(8,128)} %refs_4_.1, bf16[256,384]{1,0:T(8,128)(2,1)} %constant.12.clone.refs_5_, f32[128,128]{1,0:T(8,128)} %constant.13.clone.refs_6_, ...), custom_call_target="tpu_custom_call" | custom-call | tf_op jit(solution)/shard_map/pallas_call | solution.py:346
  46.2 0.7 %slice_bitcast_fusion = (f32[16,1024]{1,0:T(8,128)}, f32[16,1024]{1,0:T(8,128)}, f32[16,1024]{1,0:T(8,128)}, f32[16,1024]{1,0:T(8,128)}, f32[16,1024]{1,0:T(8,128)}) fusion(f32[5,16,1024]{2,1,0:T(8,128)S(1)} %shard_map.146), kind=kLoop, calls=%fused_computation | loop fusion | bytes 655360 | tf_op jit(solution)/shard_map/squeeze | solution.py:377

commit v6 on v4

--- a/solution.py
+++ b/solution.py
@@ -156,7 +156,8 @@
 
     def spread_z(phase, group, items, source, target):
         for at, step in enumerate(z_order(zs)):
-            peer = at + (lane <= at).astype(jnp.int32) if phase == 3 else z_peer(step)
+            last = phase == 3 and group == 1
+            peer = at + (lane <= at).astype(jnp.int32) if last else z_peer(step)
             pltpu.make_async_remote_copy(
                 src_ref=source.at[peer, items],
                 dst_ref=target.at[lane, items],

time: 47.3 us -> 47.2 us (level)
  no operation moved by 1% of the time
where the time goes in v6:
time: 47.2 us; the launch traced here: 46.8 us
  Pallas kernels  45.4 us (96%)
  local copies, waits for them, and re-layouts  0.72 us (2%)
  between operations  0.64 us (1%)
    pallas_call x1, Pallas kernels, per_device(): pl.pallas_call(body, out_shape=pltpu.VMEM((5, channels, tokens), jnp.floa...  45.4 us

profile of v6, /device:TPU:6, one launch (start us, length us, event | category | flops | bytes accessed | tf_op | source)
XLA Modules:
  0.0 46.8 jit_solution(14242263609144119527)
XLA Ops:
  0.6 45.4 %shard_map.146 = f32[5,16,1024]{2,1,0:T(8,128)S(1)} custom-call(f32[16,1024]{1,0:T(8,128)} %refs_0_.1, f32[16,1024]{1,0:T(8,128)} %refs_1_.1, f32[16,1024]{1,0:T(8,128)} %refs_2_.1, f32[16,1024]{1,0:T(8,128)} %refs_3_.1, f32[16,1024]{1,0:T(8,128)} %refs_4_.1, bf16[256,384]{1,0:T(8,128)(2,1)} %constant.12.clone.refs_5_, f32[128,128]{1,0:T(8,128)} %constant.13.clone.refs_6_, ...), custom_call_target="tpu_custom_call" | custom-call | tf_op jit(solution)/shard_map/pallas_call | solution.py:364
  46.1 0.7 %slice_bitcast_fusion = (f32[16,1024]{1,0:T(8,128)}, f32[16,1024]{1,0:T(8,128)}, f32[16,1024]{1,0:T(8,128)}, f32[16,1024]{1,0:T(8,128)}, f32[16,1024]{1,0:T(8,128)}) fusion(f32[5,16,1024]{2,1,0:T(8,128)S(1)} %shard_map.146), kind=kLoop, calls=%fused_computation | loop fusion | bytes 655360 | tf_op jit(solution)/shard_map/squeeze | solution.py:395
